TPU v7x, 256 devices: a whole 4x4x8 slice. The times are simulated.
256 devices in a mesh: node: 8 (over y, z_lo), gz: 32 (over z_hi, x, core).
Axes of the slice: x: 4, y: 4, z: 8 (z_hi: 4, z_lo: 2; z = z_hi * 2 + z_lo), core: 2. Of those that a mesh axis runs over, the one named last changes fastest.
Arguments:
- initial: float32 [2, 128, 128, 128], P(None, 'gz'), may hold values from -3 to 3
- feed_rate: float32 [128, 128, 128], P('gz'), may hold values from 2 to 4
Outputs:
- collocation: float32 [8, 2, 128, 128, 128], P('node', None, 'gz')
All inputs are finite; a program needn't handle non-finite values.
Results may differ from a plain program's by a relative error of at most 0.0003.
Values sent between devices are 32-bit elements; how exact they have to be, the bound alone decides.
A program may use at most 64 MiB of HBM per device.

v0:
```python
import math

import jax
import jax.numpy as jnp
from jax import lax
from jax.sharding import PartitionSpec as P

M = 8
SWEEPS = 3
STEPS = 2
JACOBI = 4


time_step = 0.1
diffuse_u = 1.0
diffuse_v = 2.0


def extended(block, sides, width):
    for axis, dim in sides:
        count = lax.axis_size(axis)
        forward = [(i, i + 1) for i in range(count - 1)]
        backward = [(target, source) for source, target in forward]
        low = lax.ppermute(
            lax.slice_in_dim(block, block.shape[dim] - width, None, axis=dim), axis, forward
        )
        high = lax.ppermute(lax.slice_in_dim(block, 0, width, axis=dim), axis, backward)
        block = jnp.concatenate([low, block, high], axis=dim)
    return block


def broadcast(x, axis, root):
    mine = lax.axis_index(axis) == root
    return lax.psum(jnp.where(mine, x, jnp.zeros_like(x)), axis)


def legendre_pair(count, point):
    before = 1.0
    current = point
    for order in range(2, count + 1):
        after = ((2.0 * order - 1.0) * point * current - (order - 1.0) * before) / order
        before = current
        current = after
    return (current, before)


def radau_value(count, point):
    high, low = legendre_pair(count, point)
    return high - low


def radau_slope(count, point):
    high, low = legendre_pair(count, point)
    lower_high, lower_low = legendre_pair(count - 1, point)
    denom = point * point - 1.0
    slope_high = count * (point * high - low) / denom
    slope_low = (count - 1.0) * (point * lower_high - lower_low) / denom
    return slope_high - slope_low


def radau_tables(node_count):
    points = [1.0]
    for index in range(1, node_count):
        guess = math.cos(2.0 * math.pi * index / (2.0 * node_count - 1.0))
        for newton_index in range(100):
            guess = guess - radau_value(node_count, guess) / radau_slope(node_count, guess)
        points.append(guess)
    points = sorted(points)
    nodes = [(value + 1.0) / 2.0 for value in points]
    table = []
    for row in range(node_count):
        table.append([0.0] * node_count)
    for column in range(node_count):
        coeffs = [1.0]
        for other in range(node_count):
            if other != column:
                factor = 1.0 / (nodes[column] - nodes[other])
                shifted = [0.0] + coeffs
                scaled = [-nodes[other] * value for value in coeffs] + [0.0]
                coeffs = [(shifted[k] + scaled[k]) * factor for k in range(len(shifted))]
        for row in range(node_count):
            total = 0.0
            for power in range(len(coeffs)):
                total = total + coeffs[power] * nodes[row] ** (power + 1) / (power + 1.0)
            table[row][column] = total
    return (nodes, table)


def neighbour_sum(padded):
    center = padded[..., 1:-1, :, :]
    total = padded[..., 2:, :, :] + padded[..., :-2, :, :]
    flat = jnp.pad(center, [(0, 0)] * (center.ndim - 2) + [(1, 1), (1, 1)])
    total = total + flat[..., 2:, 1:-1] + flat[..., :-2, 1:-1]
    total = total + flat[..., 1:-1, 2:] + flat[..., 1:-1, :-2]
    return total


def reaction(iterate, feed_rate):
    upper = 1.0 + iterate[..., 0, :, :, :]
    lower = feed_rate + iterate[..., 1, :, :, :]
    cubic = upper * upper * lower
    first = 1.0 + cubic - (feed_rate + 1.0) * upper
    second = feed_rate * upper - cubic
    return jnp.stack((first, second), axis=-4)


def on_device(initial, feed_rate):
    node_table, weight_table = radau_tables(M)
    weights = jnp.asarray(weight_table, jnp.float32)
    nodes = jnp.asarray(node_table, jnp.float32)
    local_nodes = M // lax.axis_size("node")
    position = lax.axis_index("node")
    my_rows = lax.dynamic_slice_in_dim(weights, position * local_nodes, local_nodes, 0)
    my_nodes = lax.dynamic_slice_in_dim(nodes, position * local_nodes, local_nodes, 0)
    diffusion = jnp.asarray([diffuse_u, diffuse_v], jnp.float32)[:, None, None, None]
    anchor = initial
    iterate = jnp.broadcast_to(anchor, (local_nodes,) + anchor.shape)
    for step_index in range(STEPS):
        iterate = jnp.broadcast_to(anchor, (local_nodes,) + anchor.shape)
        for sweep_index in range(SWEEPS):
            stiffness = (my_nodes / (sweep_index + 1.0))[:, None, None, None, None] * diffusion
            padded = extended(iterate, (("gz", 2),), 1)
            laplace = neighbour_sum(padded) - 6.0 * iterate
            slopes = diffusion * laplace + time_step * reaction(iterate, feed_rate)
            pieces = lax.all_gather(slopes, "node", axis=0, tiled=True)
            columns = lax.slice_in_dim(my_rows, 0, pieces.shape[0], axis=1)
            integral = jnp.zeros_like(slopes) + jnp.einsum(
                "mj,jsabc->msabc", columns, pieces, precision=lax.Precision.HIGHEST
            )
            right_side = anchor + integral - stiffness * laplace
            scale = 1.0 + 6.0 * stiffness
            current = (right_side + stiffness * neighbour_sum(padded)) / scale
            for jacobi_index in range(1, JACOBI):
                beside_all = extended(current, (("gz", 2),), 1)
                current = (right_side + stiffness * neighbour_sum(beside_all)) / scale
            iterate = current
        if step_index + 1 < STEPS:
            anchor = broadcast(iterate[local_nodes - 1], "node", lax.axis_size("node") - 1)
    return iterate


def solution(mesh):
    in_specs = (P(None, "gz", None, None), P("gz", None, None))
    out_specs = P("node", None, "gz", None, None)
    return jax.shard_map(
        on_device, mesh=mesh, in_specs=in_specs, out_specs=out_specs, check_vma=False
    )
```

profile of v0, /device:TPU:128, one launch (start us, length us, event | category | flops | bytes accessed | tf_op | source)
XLA Modules:
  0.0 1040.7 jit_solution(11607115618912697490)
XLA Ops:
  13.9 8.1 collective-permute-done.1
  28.6 90.2 %all-gather.7.cloned.1.call-done = f32[8,2,4,128,128]{4,3,2,1,0:T(8,128)} async-done(((f32[1,2,4,128,128]{4,3,2,1,0:T(8,128)}), f32[8,2,4,128,128]{4,3,2,1,0:T(8,128)}) %all-gather.7.cloned.1.call-update) | async-done | bytes 4194320 | tf_op jit(solution)/shard_map/all_gather | solution.py:125
  118.8 8.1 fusion.10
  147.7 8.1 collective-permute-done.5
  160.6 8.0 collective-permute-done.7
  182.8 92.4 %all-gather.9.cloned.1.call-done = f32[8,2,4,128,128]{4,3,2,1,0:T(8,128)} async-done(((f32[1,2,4,128,128]{4,3,2,1,0:T(8,128)}), f32[8,2,4,128,128]{4,3,2,1,0:T(8,128)}) %all-gather.9.cloned.1.call-update) | async-done | bytes 4194320 | tf_op jit(solution)/shard_map/all_gather | solution.py:125
  275.2 8.1 fusion.8
  304.0 8.1 collective-permute-done.13
  316.9 8.0 collective-permute-done.15
  339.1 92.4 %all-gather.11.cloned.1.call-done = f32[8,2,4,128,128]{4,3,2,1,0:T(8,128)} async-done(((f32[1,2,4,128,128]{4,3,2,1,0:T(8,128)}), f32[8,2,4,128,128]{4,3,2,1,0:T(8,128)}) %all-gather.11.cloned.1.call-update) | async-done | bytes 4194320 | tf_op jit(solution)/shard_map/all_gather | solution.py:125
  431.5 8.1 fusion.6
  460.3 8.1 collective-permute-done.21
  473.2 8.0 collective-permute-done.23
  482.4 79.5 %all-reduce.26.cloned.1.call-done = f32[2,4,128,128]{3,2,1,0:T(8,128)} async-done(((f32[2,4,128,128]{3,2,1,0:T(8,128)}), f32[2,4,128,128]{3,2,1,0:T(8,128)}) %all-reduce.26.cloned.1.call-update) | async-done | bytes 524304 | tf_op jit(solution)/shard_map/psum | solution.py:34
  579.4 90.8 %all-gather.13.cloned.1.call-done = f32[8,2,4,128,128]{4,3,2,1,0:T(8,128)} async-done(((f32[1,2,4,128,128]{4,3,2,1,0:T(8,128)}), f32[8,2,4,128,128]{4,3,2,1,0:T(8,128)}) %all-gather.13.cloned.1.call-update) | async-done | bytes 4194320 | tf_op jit(solution)/shard_map/all_gather | solution.py:125
  670.2 8.1 fusion.4
  698.9 8.1 collective-permute-done.29
  711.8 8.0 collective-permute-done.31
  734.3 92.1 %all-gather.15.cloned.1.call-done = f32[8,2,4,128,128]{4,3,2,1,0:T(8,128)} async-done(((f32[1,2,4,128,128]{4,3,2,1,0:T(8,128)}), f32[8,2,4,128,128]{4,3,2,1,0:T(8,128)}) %all-gather.15.cloned.1.call-update) | async-done | bytes 4194320 | tf_op jit(solution)/shard_map/all_gather | solution.py:125
  826.5 8.1 fusion.2
  855.2 8.1 collective-permute-done.37
  890.1 92.6 %all-gather.17.cloned.1.call-done = f32[8,2,4,128,128]{4,3,2,1,0:T(8,128)} async-done(((f32[1,2,4,128,128]{4,3,2,1,0:T(8,128)}), f32[8,2,4,128,128]{4,3,2,1,0:T(8,128)}) %all-gather.17.cloned.1.call-update) | async-done | bytes 4194320 | tf_op jit(solution)/shard_map/all_gather | solution.py:125
  982.8 8.1 fusion
  1011.6 8.1 collective-permute-done.45
  (173 shorter events, 257.3 us)
Async XLA Ops:
  6.5 112.2 %all-gather.7.cloned.1.call-start = ((), (), s32[]{:S(2)}) async-start(), calls=%async_computation | async-start | bytes 4718592 | tf_op jit(solution)/shard_map/all_gather | solution.py:125
  10.8 11.3 %collective-permute-start.1 = (f32[1,2,1,128,128]{4,3,2,1,0:T(8,128)S(1)}, f32[1,2,1,128,128]{4,3,2,1,0:T(8,128)S(1)}, u32[]{:S(2)}, u32[]{:S(2)}) collective-permute-start(f32[1,2,1,128,128]{4,3,2,1,0:T(8,128)S(1)} %get-tuple-element.88), channel_id=1, source_target_pairs={{0,1},{1,2},{2,3},{3,4},{4,5},{5,6},{6,7},{7,8},{8,9},{9,10},{10,1... | collective-permute-start | bytes 393224 | tf_op jit(solution)/shard_map/ppermute | solution.py:24
  26.0 249.1 %all-gather.9.cloned.1.call-start = ((), (), s32[]{:S(2)}) async-start(), calls=%async_computation.1 | async-start | bytes 4718592 | tf_op jit(solution)/shard_map/all_gather | solution.py:125
  131.9 10.9 %collective-permute-start.3 = (f32[1,2,1,128,128]{4,3,2,1,0:T(8,128)S(1)}, f32[1,2,1,128,128]{4,3,2,1,0:T(8,128)S(1)}, u32[]{:S(2)}, u32[]{:S(2)}) collective-permute-start(f32[1,2,1,128,128]{4,3,2,1,0:T(8,128)S(1)} %get-tuple-element.86), channel_id=1, source_target_pairs={{0,1},{1,2},{2,3},{3,4},{4,5},{5,6},{6,7},{7,8},{8,9},{9,10},{10,1... | collective-permute-start | bytes 393224 | tf_op jit(solution)/shard_map/ppermute | solution.py:24
  145.1 10.6 %collective-permute-start.5 = (f32[1,2,1,128,128]{4,3,2,1,0:T(8,128)S(1)}, f32[1,2,1,128,128]{4,3,2,1,0:T(8,128)S(1)}, u32[]{:S(2)}, u32[]{:S(2)}) collective-permute-start(f32[1,2,1,128,128]{4,3,2,1,0:T(8,128)S(1)} %get-tuple-element.84), channel_id=1, source_target_pairs={{0,1},{1,2},{2,3},{3,4},{4,5},{5,6},{6,7},{7,8},{8,9},{9,10},{10,1... | collective-permute-start | bytes 393224 | tf_op jit(solution)/shard_map/ppermute | solution.py:24
  158.1 10.5 %collective-permute-start.7 = (f32[1,2,1,128,128]{4,3,2,1,0:T(8,128)S(1)}, f32[1,2,1,128,128]{4,3,2,1,0:T(8,128)S(1)}, u32[]{:S(2)}, u32[]{:S(2)}) collective-permute-start(f32[1,2,1,128,128]{4,3,2,1,0:T(8,128)S(1)} %get-tuple-element.82), channel_id=1, source_target_pairs={{0,1},{1,2},{2,3},{3,4},{4,5},{5,6},{6,7},{7,8},{8,9},{9,10},{10,1... | collective-permute-start | bytes 393224 | tf_op jit(solution)/shard_map/ppermute | solution.py:24
  182.6 248.9 %all-gather.11.cloned.1.call-start = ((), (), s32[]{:S(2)}) async-start(), calls=%async_computation.2 | async-start | bytes 4718592 | tf_op jit(solution)/shard_map/all_gather | solution.py:125
  288.2 10.9 %collective-permute-start.11 = (f32[1,2,1,128,128]{4,3,2,1,0:T(8,128)S(1)}, f32[1,2,1,128,128]{4,3,2,1,0:T(8,128)S(1)}, u32[]{:S(2)}, u32[]{:S(2)}) collective-permute-start(f32[1,2,1,128,128]{4,3,2,1,0:T(8,128)S(1)} %get-tuple-element.78), channel_id=1, source_target_pairs={{0,1},{1,2},{2,3},{3,4},{4,5},{5,6},{6,7},{7,8},{8,9},{9,10},{10,1... | collective-permute-start | bytes 393224 | tf_op jit(solution)/shard_map/ppermute | solution.py:24
  301.4 10.6 %collective-permute-start.13 = (f32[1,2,1,128,128]{4,3,2,1,0:T(8,128)S(1)}, f32[1,2,1,128,128]{4,3,2,1,0:T(8,128)S(1)}, u32[]{:S(2)}, u32[]{:S(2)}) collective-permute-start(f32[1,2,1,128,128]{4,3,2,1,0:T(8,128)S(1)} %get-tuple-element.76), channel_id=1, source_target_pairs={{0,1},{1,2},{2,3},{3,4},{4,5},{5,6},{6,7},{7,8},{8,9},{9,10},{10,1... | collective-permute-start | bytes 393224 | tf_op jit(solution)/shard_map/ppermute | solution.py:24
  314.4 10.5 %collective-permute-start.15 = (f32[1,2,1,128,128]{4,3,2,1,0:T(8,128)S(1)}, f32[1,2,1,128,128]{4,3,2,1,0:T(8,128)S(1)}, u32[]{:S(2)}, u32[]{:S(2)}) collective-permute-start(f32[1,2,1,128,128]{4,3,2,1,0:T(8,128)S(1)} %get-tuple-element.74), channel_id=1, source_target_pairs={{0,1},{1,2},{2,3},{3,4},{4,5},{5,6},{6,7},{7,8},{8,9},{9,10},{10,1... | collective-permute-start | bytes 393224 | tf_op jit(solution)/shard_map/ppermute | solution.py:24
  338.9 223.0 %all-reduce.26.cloned.1.call-start = ((), (), s32[]{:S(2)}) async-start(), calls=%async_computation.3 | async-start | bytes 1048576 | tf_op jit(solution)/shard_map/psum | solution.py:34
  444.5 10.9 %collective-permute-start.19 = (f32[1,2,1,128,128]{4,3,2,1,0:T(8,128)S(1)}, f32[1,2,1,128,128]{4,3,2,1,0:T(8,128)S(1)}, u32[]{:S(2)}, u32[]{:S(2)}) collective-permute-start(f32[1,2,1,128,128]{4,3,2,1,0:T(8,128)S(1)} %get-tuple-element.70), channel_id=1, source_target_pairs={{0,1},{1,2},{2,3},{3,4},{4,5},{5,6},{6,7},{7,8},{8,9},{9,10},{10,1... | collective-permute-start | bytes 393224 | tf_op jit(solution)/shard_map/ppermute | solution.py:24
  457.7 10.6 %collective-permute-start.21 = (f32[1,2,1,128,128]{4,3,2,1,0:T(8,128)S(1)}, f32[1,2,1,128,128]{4,3,2,1,0:T(8,128)S(1)}, u32[]{:S(2)}, u32[]{:S(2)}) collective-permute-start(f32[1,2,1,128,128]{4,3,2,1,0:T(8,128)S(1)} %get-tuple-element.68), channel_id=1, source_target_pairs={{0,1},{1,2},{2,3},{3,4},{4,5},{5,6},{6,7},{7,8},{8,9},{9,10},{10,1... | collective-permute-start | bytes 393224 | tf_op jit(solution)/shard_map/ppermute | solution.py:24
  470.7 10.5 %collective-permute-start.23 = (f32[1,2,1,128,128]{4,3,2,1,0:T(8,128)S(1)}, f32[1,2,1,128,128]{4,3,2,1,0:T(8,128)S(1)}, u32[]{:S(2)}, u32[]{:S(2)}) collective-permute-start(f32[1,2,1,128,128]{4,3,2,1,0:T(8,128)S(1)} %get-tuple-element.66), channel_id=1, source_target_pairs={{0,1},{1,2},{2,3},{3,4},{4,5},{5,6},{6,7},{7,8},{8,9},{9,10},{10,1... | collective-permute-start | bytes 393224 | tf_op jit(solution)/shard_map/ppermute | solution.py:24
  482.3 187.8 %all-gather.13.cloned.1.call-start = ((), (), s32[]{:S(2)}) async-start(), calls=%async_computation.4 | async-start | bytes 4718592 | tf_op jit(solution)/shard_map/all_gather | solution.py:125
  579.1 247.4 %all-gather.15.cloned.1.call-start = ((), (), s32[]{:S(2)}) async-start(), calls=%async_computation.5 | async-start | bytes 4718592 | tf_op jit(solution)/shard_map/all_gather | solution.py:125
  683.2 10.9 %collective-permute-start.27 = (f32[1,2,1,128,128]{4,3,2,1,0:T(8,128)S(1)}, f32[1,2,1,128,128]{4,3,2,1,0:T(8,128)S(1)}, u32[]{:S(2)}, u32[]{:S(2)}) collective-permute-start(f32[1,2,1,128,128]{4,3,2,1,0:T(8,128)S(1)} %get-tuple-element.62), channel_id=1, source_target_pairs={{0,1},{1,2},{2,3},{3,4},{4,5},{5,6},{6,7},{7,8},{8,9},{9,10},{10,1... | collective-permute-start | bytes 393224 | tf_op jit(solution)/shard_map/ppermute | solution.py:24
  696.4 10.6 %collective-permute-start.29 = (f32[1,2,1,128,128]{4,3,2,1,0:T(8,128)S(1)}, f32[1,2,1,128,128]{4,3,2,1,0:T(8,128)S(1)}, u32[]{:S(2)}, u32[]{:S(2)}) collective-permute-start(f32[1,2,1,128,128]{4,3,2,1,0:T(8,128)S(1)} %get-tuple-element.60), channel_id=1, source_target_pairs={{0,1},{1,2},{2,3},{3,4},{4,5},{5,6},{6,7},{7,8},{8,9},{9,10},{10,1... | collective-permute-start | bytes 393224 | tf_op jit(solution)/shard_map/ppermute | solution.py:24
  709.3 10.5 %collective-permute-start.31 = (f32[1,2,1,128,128]{4,3,2,1,0:T(8,128)S(1)}, f32[1,2,1,128,128]{4,3,2,1,0:T(8,128)S(1)}, u32[]{:S(2)}, u32[]{:S(2)}) collective-permute-start(f32[1,2,1,128,128]{4,3,2,1,0:T(8,128)S(1)} %get-tuple-element.58), channel_id=1, source_target_pairs={{0,1},{1,2},{2,3},{3,4},{4,5},{5,6},{6,7},{7,8},{8,9},{9,10},{10,1... | collective-permute-start | bytes 393224 | tf_op jit(solution)/shard_map/ppermute | solution.py:24
  733.8 248.9 %all-gather.17.cloned.1.call-start = ((), (), s32[]{:S(2)}) async-start(), calls=%async_computation.6 | async-start | bytes 4718592 | tf_op jit(solution)/shard_map/all_gather | solution.py:125
  839.5 10.9 %collective-permute-start.35 = (f32[1,2,1,128,128]{4,3,2,1,0:T(8,128)S(1)}, f32[1,2,1,128,128]{4,3,2,1,0:T(8,128)S(1)}, u32[]{:S(2)}, u32[]{:S(2)}) collective-permute-start(f32[1,2,1,128,128]{4,3,2,1,0:T(8,128)S(1)} %get-tuple-element.54), channel_id=1, source_target_pairs={{0,1},{1,2},{2,3},{3,4},{4,5},{5,6},{6,7},{7,8},{8,9},{9,10},{10,1... | collective-permute-start | bytes 393224 | tf_op jit(solution)/shard_map/ppermute | solution.py:24
  852.7 10.6 %collective-permute-start.37 = (f32[1,2,1,128,128]{4,3,2,1,0:T(8,128)S(1)}, f32[1,2,1,128,128]{4,3,2,1,0:T(8,128)S(1)}, u32[]{:S(2)}, u32[]{:S(2)}) collective-permute-start(f32[1,2,1,128,128]{4,3,2,1,0:T(8,128)S(1)} %get-tuple-element.52), channel_id=1, source_target_pairs={{0,1},{1,2},{2,3},{3,4},{4,5},{5,6},{6,7},{7,8},{8,9},{9,10},{10,1... | collective-permute-start | bytes 393224 | tf_op jit(solution)/shard_map/ppermute | solution.py:24
  995.8 10.9 %collective-permute-start.43 = (f32[1,2,1,128,128]{4,3,2,1,0:T(8,128)S(1)}, f32[1,2,1,128,128]{4,3,2,1,0:T(8,128)S(1)}, u32[]{:S(2)}, u32[]{:S(2)}) collective-permute-start(f32[1,2,1,128,128]{4,3,2,1,0:T(8,128)S(1)} %get-tuple-element.46), channel_id=1, source_target_pairs={{0,1},{1,2},{2,3},{3,4},{4,5},{5,6},{6,7},{7,8},{8,9},{9,10},{10,1... | collective-permute-start | bytes 393224 | tf_op jit(solution)/shard_map/ppermute | solution.py:24
  1009.0 10.6 %collective-permute-start.45 = (f32[1,2,1,128,128]{4,3,2,1,0:T(8,128)S(1)}, f32[1,2,1,128,128]{4,3,2,1,0:T(8,128)S(1)}, u32[]{:S(2)}, u32[]{:S(2)}) collective-permute-start(f32[1,2,1,128,128]{4,3,2,1,0:T(8,128)S(1)} %get-tuple-element.44), channel_id=1, source_target_pairs={{0,1},{1,2},{2,3},{3,4},{4,5},{5,6},{6,7},{7,8},{8,9},{9,10},{10,1... | collective-permute-start | bytes 393224 | tf_op jit(solution)/shard_map/ppermute | solution.py:24
  (37 other events, 629.7 us)
Sparse Core Ops, SparseCore 0:
  26.2 92.5 all-gather.6
  182.7 92.4 all-gather.8
  339.0 92.4 all-gather.10
  482.5 79.3 all-reduce.25
  579.2 90.9 all-gather.12
  733.9 92.4 all-gather.14
  890.3 92.4 all-gather.16
where the time goes:
time: 1050 us; the launch traced here: 1040 us
  waiting for transfers between devices  829 us (79%)
  starting transfers between devices  119 us (11%)
  matrix products  48.9 us (5%)
  other arithmetic  25.2 us (2%)
  between operations  15.9 us (2%)
    all_gather x6, waiting for transfers between devices, on_device(): pieces = lax.all_gather(slopes, 'node', axis=0, tiled=True)  550 us
    ppermute x24, waiting for transfers between devices, extended(): lax.ppermute(lax.slice_in_dim(block, block.shape[dim] - width, None, axis...  186 us
    psum x1, waiting for transfers between devices, broadcast(): return lax.psum(jnp.where(mine, x, jnp.zeros_like(x)), axis)  79.5 us
    ppermute x24, starting transfers between devices, extended(): lax.ppermute(lax.slice_in_dim(block, 0, width, axis=dim), axis, backward)  63.2 us
    ppermute x24, starting transfers between devices, extended(): lax.ppermute(lax.slice_in_dim(block, block.shape[dim] - width, None, axis...  54.5 us
    dot_general x6, matrix products, on_device(): jnp.einsum('mj,jsabc->msabc', columns, pieces, precision=lax.Precision.HI...  48.9 us
  transfers between devices with their start and end apart: 55, of which 49 were waited for; matrix products, arithmetic and copies ran while one was open for 0% of the time, Pallas kernels for 0%

commit v1 on v0

v1 whole, which is shorter than its diff:
```python
import math

import jax
import jax.numpy as jnp
import ml_dtypes
import numpy as np
from jax import lax
from jax.experimental import pallas as pl
from jax.experimental.pallas import tpu as pltpu
from jax.sharding import PartitionSpec as P

MESH = pl.DeviceIdType.MESH
M = 8
SLABS, STRIPS = 32, 8
OWN_Z, OWN_X = 4, 16
Z_AT, X_AT = 12, 16
WIDE = 128


def legendre_pair(count, point):
    before = 1.0
    current = point
    for order in range(2, count + 1):
        after = ((2.0 * order - 1.0) * point * current - (order - 1.0) * before) / order
        before = current
        current = after
    return (current, before)


def radau_value(count, point):
    high, low = legendre_pair(count, point)
    return high - low


def radau_slope(count, point):
    high, low = legendre_pair(count, point)
    lower_high, lower_low = legendre_pair(count - 1, point)
    denom = point * point - 1.0
    slope_high = count * (point * high - low) / denom
    slope_low = (count - 1.0) * (point * lower_high - lower_low) / denom
    return slope_high - slope_low


def radau_tables(node_count):
    points = [1.0]
    for index in range(1, node_count):
        guess = math.cos(2.0 * math.pi * index / (2.0 * node_count - 1.0))
        for newton_index in range(100):
            guess = guess - radau_value(node_count, guess) / radau_slope(node_count, guess)
        points.append(guess)
    points = sorted(points)
    nodes = [(value + 1.0) / 2.0 for value in points]
    table = []
    for row in range(node_count):
        table.append([0.0] * node_count)
    for column in range(node_count):
        coeffs = [1.0]
        for other in range(node_count):
            if other != column:
                factor = 1.0 / (nodes[column] - nodes[other])
                shifted = [0.0] + coeffs
                scaled = [-nodes[other] * value for value in coeffs] + [0.0]
                coeffs = [(shifted[k] + scaled[k]) * factor for k in range(len(shifted))]
        for row in range(node_count):
            total = 0.0
            for power in range(len(coeffs)):
                total = total + coeffs[power] * nodes[row] ** (power + 1) / (power + 1.0)
            table[row][column] = total
    return (nodes, table)


def tables():
    nodes, weights = radau_tables(M)
    t, q = np.asarray(nodes), np.asarray(weights)
    k = np.arange(1, WIDE + 1)
    sine = np.sqrt(2.0 / (WIDE + 1)) * np.sin(np.pi * np.outer(k, k) / (WIDE + 1))
    index, rows = {}, []

    def add(name, column):
        index[name] = len(rows)
        rows.append(np.broadcast_to(column[:, None], (8, WIDE)))

    index["lam"] = 0
    rows.append(np.broadcast_to(2.0 * np.cos(np.pi * k / (WIDE + 1))[None, :], (8, WIDE)))
    for s, nu in ((0, 1.0), (1, 2.0)):
        c = t * nu
        i = 1.0 / (1.0 + 6.0 * c)
        a = c * i
        for p in range(4):
            add(("A", s, p), a**p * i * ((1.0 - 0.1 * t) if s == 0 else 1.0))
            add(("N", s, p), a**p * i * t * (1.0 if s == 0 else -1.0))
        add(("A", s, 4), a**4)
        for sweep in (2, 3):
            c = t * nu / sweep
            i = 1.0 / (1.0 + 6.0 * c)
            add(("c", s, sweep), c)
            add(("i", s, sweep), i)
            add(("a", s, sweep), c * i)
    for j in range(M):
        add(("q", j), q[:, j])
    return np.concatenate(rows, 0).astype(np.float32), index, sine


COEF, INDEX, SINE = tables()


def wide(matrix):
    high = matrix.astype(ml_dtypes.bfloat16)
    low = (matrix - high.astype(np.float64)).astype(ml_dtypes.bfloat16)
    return np.block([[high, low], [high, np.zeros_like(low)]]).astype(ml_dtypes.bfloat16)


def transform(v, matrix):
    high = v.astype(jnp.bfloat16)
    low = (v - high.astype(jnp.float32)).astype(jnp.bfloat16)
    both = jnp.dot(jnp.concatenate([high, low], 1), matrix[...], preferred_element_type=jnp.float32)
    return both[:, :WIDE] + both[:, WIDE:]


def total(terms):
    while len(terms) > 1:
        odd = [terms[-1]] if len(terms) % 2 else []
        terms = [terms[i] + terms[i + 1] for i in range(0, len(terms) - 1, 2)] + odd
    return terms[0]


class Stack:
    def __init__(self, ref, z0, nz, x0, nx):
        self.ref, self.z0, self.nz, self.x0, self.nx = ref, z0, nz, x0, nx

    def at(self, s, z, x):
        return pl.multiple_of(((s * self.nz + (z - self.z0)) * self.nx + (x - self.x0)) * 8, 8)

    def get(self, s, z, x):
        return self.ref[pl.ds(self.at(s, z, x), 8), :]

    def put(self, s, z, x, v):
        self.ref[pl.ds(self.at(s, z, x), 8), :] = v

    def row(self, s, z, x, f):
        return jnp.broadcast_to(self.ref[pl.ds(self.at(s, z, x) + f, 1), :], (8, WIDE))

    def line(self, s, z, x, n):
        return self.ref[pl.ds(self.at(s, z, x), n * 8), :]


def span(depth):
    return (Z_AT - depth, OWN_Z + 2 * depth, X_AT - depth, OWN_X + 2 * depth)


def volume(depth):
    return 2 * (OWN_Z + 2 * depth) * (OWN_X + 2 * depth) * 8


class Device:
    def __init__(self, refs, g, k):
        self.__dict__.update(refs)
        self.g, self.k = g, k

    def co(self, name):
        i = INDEX[name]
        return self.coef[i * 8 : (i + 1) * 8, :]

    def zero_edges(self, stack, parts):
        for edge, x in ((0, X_AT - 1), (STRIPS - 1, X_AT + OWN_X)):

            @pl.when(self.k == edge)
            def _():
                def body(z, _):
                    for s in range(parts):
                        stack.put(s, z, x, jnp.zeros((8, WIDE), jnp.float32))
                    return 0

                lax.fori_loop(stack.z0, stack.z0 + stack.nz, body, 0)

        for i in range(3):
            for edge, z in ((i, Z_AT - 4 * i - 1), (SLABS - 1 - i, Z_AT + OWN_Z + 4 * i)):
                if stack.z0 <= z < stack.z0 + stack.nz:

                    @pl.when(self.g == edge)
                    def _():
                        for s in range(parts):
                            stack.ref[pl.ds(stack.at(s, z, stack.x0), stack.nx * 8), :] = jnp.zeros(
                                (stack.nx * 8, WIDE), jnp.float32
                            )

    def load(self, blocks, first, stack):
        def body(slot, _):
            b = slot * 3
            x = jnp.concatenate([blocks[b + i, 0:2].reshape(128, WIDE) for i in range(3)], 0)
            y = transform(x, self.sine)
            real, spec = (x, y) if first else (y, x)
            n = []
            for i in range(3):
                p, q = real[i * 128 : i * 128 + 64], real[i * 128 + 64 : i * 128 + 128]
                feed = self.held[b + i, 2].reshape(64, WIDE)
                n.append((1.0 + p) * (q + p * (feed + q)))
            n = transform(jnp.concatenate(n, 0), self.sine_tenth)
            for i in range(3):
                for layer in range(4):
                    for t in range(2):
                        at = stack.at(0, slot * 4 + layer, i * 16 + t * 8)
                        r = layer * 16 + t * 8
                        for f, v in (
                            (0, spec[i * 128 + r : i * 128 + r + 8]),
                            (1, spec[i * 128 + 64 + r : i * 128 + 64 + r + 8]),
                            (2, n[i * 64 + r : i * 64 + r + 8]),
                        ):
                            stack.ref[pl.ds(at + f, 8, stride=8), :] = v
            return 0

        lax.fori_loop(0, 7, body, 0)

    def apply_s(self, src, dst):
        lam = self.co("lam")

        def body(z, _):
            for x0 in range(dst.x0, dst.x0 + dst.nx, 8):
                xs = range(x0, min(x0 + 8, dst.x0 + dst.nx))
                row = {x: src.get(0, z, x) for x in range(xs[0] - 1, xs[-1] + 2)}
                for x in xs:
                    zx = (row[x - 1] + row[x + 1]) + (src.get(0, z - 1, x) + src.get(0, z + 1, x))
                    dst.put(0, z, x, zx + lam * row[x])
            return 0

        lax.fori_loop(dst.z0, dst.z0 + dst.nz, body, 0)

    def combine(self, powers, out):
        ca = [[self.co(("A", s, p)) for p in range(5)] for s in range(2)]
        cn = [[self.co(("N", s, p)) for p in range(4)] for s in range(2)]

        def body(z, _):
            for x in range(out.x0, out.x0 + out.nx):
                n = [powers[p].row(0, z, x, 2) for p in range(4)]
                for s in range(2):
                    terms = [ca[s][p] * powers[p].row(0, z, x, s) for p in range(5)]
                    out.put(s, z, x, total(terms + [cn[s][p] * n[p] for p in range(4)]))
            return 0

        lax.fori_loop(out.z0, out.z0 + out.nz, body, 0)

    def rates(self, u, anchor, right, out, sweep):
        lam = self.co("lam")
        a, c, inv = [[self.co((name, s, sweep)) for s in range(2)] for name in "aci"]
        weights = [self.co(("q", j)) for j in range(M)]
        nx, x0 = right.nx, right.x0
        lam6, lam61 = lam - 6.0, lam - 6.1
        rate = Stack(self.rate, 0, 2, x0, nx)

        def body(i, _):
            z0 = right.z0 + 2 * i
            real = transform(
                jnp.concatenate([u.line(s, z0 + w, x0, nx) for s in range(2) for w in range(2)], 0), self.sine
            )
            feed = []
            for w in range(2):
                z = z0 + w
                for x in range(x0, x0 + nx):
                    line = self.held[(z // 4) * 3 + x // 16, 2, z % 4, pl.ds(x % 16, 1), :]
                    feed.append(jnp.broadcast_to(line, (8, WIDE)))
            feed = jnp.concatenate(feed, 0)
            p, q = real[: 2 * nx * 8], real[2 * nx * 8 :]
            self.modes[0 : 2 * nx * 8, :] = transform((1.0 + p) * (q + p * (feed + q)), self.sine_tenth)
            for w in range(2):
                z = z0 + w
                for x in range(x0, x0 + nx):
                    shifted, laplace = [], []
                    for s in range(2):
                        own = u.get(s, z, x)
                        zx = (u.get(s, z, x - 1) + u.get(s, z, x + 1)) + (u.get(s, z - 1, x) + u.get(s, z + 1, x))
                        shifted.append(zx + lam * own)
                        laplace.append(zx + lam6 * own)
                        if s == 0:
                            drift = zx + lam61 * own
                    at = (w * nx + x - x0) * 8
                    n = self.modes[at : at + 8, :]
                    rate.put(0, w, x, drift + n)
                    rate.put(1, w, x, 2.0 * laplace[1] - n)
                    for s in range(2):
                        integral = total([weights[j] * rate.row(s, w, x, j) for j in range(M)])
                        r = inv[s] * ((anchor.row(0, z, x, s) - c[s] * laplace[s]) + integral)
                        right.put(s, z, x, r)
                        out.put(s, z, x, r + a[s] * shifted[s])
            return 0

        lax.fori_loop(0, right.nz // 2, body, 0)

    def jacobi(self, src, right, dst, sweep):
        lam = self.co("lam")
        a = [self.co(("a", s, sweep)) for s in range(2)]

        def body(z, _):
            for x0 in range(dst.x0, dst.x0 + dst.nx, 7):
                xs = range(x0, min(x0 + 7, dst.x0 + dst.nx))
                for s in range(2):
                    row = {x: src.get(s, z, x) for x in range(xs[0] - 1, xs[-1] + 2)}
                    for x in xs:
                        zx = (row[x - 1] + row[x + 1]) + (src.get(s, z - 1, x) + src.get(s, z + 1, x))
                        dst.put(s, z, x, right.get(s, z, x) + a[s] * (zx + lam * row[x]))
            return 0

        lax.fori_loop(dst.z0, dst.z0 + dst.nz, body, 0)

    def step(self, blocks, first):
        powers = [Stack(self.power[0], 0, 28, 0, 48)]
        powers += [Stack(self.power[i], i, 28 - 2 * i, 4 + i, 40 - 2 * i) for i in range(1, 5)]
        self.load(blocks, first, powers[0])
        for i in range(4):
            self.zero_edges(powers[i], 1)
            self.apply_s(powers[i], powers[i + 1])
        u = Stack(self.state[0], *span(8))
        self.combine(powers, u)
        for sweep, depth in ((2, 8), (3, 4)):
            right, out = Stack(self.state[1], *span(depth - 1)), Stack(self.state[2], *span(depth - 1))
            self.zero_edges(u, 2)
            self.rates(u, powers[0], right, out, sweep)
            for d, place in ((depth - 2, 3), (depth - 3, 2), (depth - 4, 3)):
                u = Stack(self.state[place], *span(d))
                self.zero_edges(out, 2)
                self.jacobi(out, right, u, sweep)
                out = u
        return u


def strip_of(node):
    y = node // 2
    return 2 * y + (node + y) % 2


class Links:
    def __init__(self):
        self.sent = []

    def send(self, when, copy):
        @pl.when(when)
        def _():
            copy.start()

        self.sent.append((when, copy))

    def finish(self):
        for when, copy in self.sent:

            @pl.when(when)
            def _():
                copy.wait_send()


def remote(src, dst, sent, got, node, g):
    return pltpu.make_async_remote_copy(
        src_ref=src, dst_ref=dst, send_sem=sent, recv_sem=got, device_id=(node, g), device_id_type=MESH
    )


def arrive(when, copy):
    @pl.when(when)
    def _():
        copy.wait_recv()


def exchange(held, sems, n, g, k, own_parts, strips_too):
    zs, zr, xs, xr, ss, sr = sems
    links = Links()
    tau = 2 * (g % 2) - 1
    partner = g - tau
    low, high = k > 0, k < STRIPS - 1

    def inside(i):
        return jnp.logical_and(i >= 0, i < SLABS)

    def block(slot, strip):
        return held.at[slot * 3 + strip]

    for d, away in ((1, tau), (2, -2 * tau), (3, 3 * tau)):
        for i, (src, part) in enumerate(own_parts):
            dst = held.at[(3 - away) * 3 + 1, part]
            copy = remote(src, dst, zs.at[d - 1, i], zr.at[d - 1, i], n, g + away)
            links.send(inside(g + away), copy)

    def along_x(j, there):
        slot = 3 + tau * j
        for way, (ok, to, strip) in enumerate(((high, k + 1, 0), (low, k - 1, 2))):
            copy = remote(block(slot, 1), block(slot, strip), xs.at[j, way], xr.at[j, way], strip_of(to), g)
            links.send(jnp.logical_and(ok, there), copy)

    def swap(j, strip, there):
        copy = remote(
            block(3 + tau * j, strip), block(3 + tau * (j + 1), strip), ss.at[j, strip], sr.at[j, strip], n, partner
        )
        links.send(there, copy)

    always = g >= 0
    swap(0, 1, always)
    if strips_too:
        along_x(0, always)
    else:
        swap(0, 0, low)
        swap(0, 2, high)
    for j in (1, 2, 3):
        there = inside(g + tau * j)
        slot = 3 + tau * j
        for i, (src, part) in enumerate(own_parts):
            arrive(there, remote(src, held.at[slot * 3 + 1, part], zs.at[j - 1, i], zr.at[j - 1, i], n, partner))
        along_x(j, there)
        if j < 3:
            swap(j, 1, there)
    for j in (0, 1, 2, 3):
        there = inside(g + tau * j)
        slot = 3 + tau * j
        for way, (ok, strip) in enumerate(((low, 0), (high, 2))):
            when = jnp.logical_and(ok, there)
            if j > 0 or strips_too:
                arrive(when, remote(block(slot, strip), block(slot, strip), xs.at[j, way], xr.at[j, way], n, partner))
                if j < 3:
                    swap(j, strip, when)
    for j in (0, 1, 2):
        there = inside(g - tau * (j + 1))
        for strip, ok in ((0, low), (1, always), (2, high)):
            slot = 3 - tau * (j + 1)
            got = remote(block(slot, strip), block(slot, strip), ss.at[j, strip], sr.at[j, strip], n, partner)
            arrive(jnp.logical_and(ok, there), got)
    links.finish()


def kernel(initial, feed, sine, sine_tenth, coef, out, held, later, rows, sending, *scratch):
    power, state, (rate, modes), sems = scratch[0:5], scratch[5:9], scratch[9:11], scratch[11:]
    own_sem, first_sems, second_sems, (send_sem, recv_sem) = sems[0], sems[1:7], sems[7:13], sems[13:15]
    n, g = lax.axis_index("node"), lax.axis_index("gz")
    k = strip_of(n)
    tau = 2 * (g % 2) - 1

    barrier = pltpu.get_barrier_semaphore()
    count = M - 1
    for j in range(1, M):
        pl.semaphore_signal(barrier, inc=1, device_id=((n + j) % M, g), device_id_type=MESH)
    for away in (-2 * tau, -tau, tau, 2 * tau, 3 * tau):
        there = jnp.logical_and(g + away >= 0, g + away < SLABS)
        count = count + jnp.where(there, 1, 0)

        @pl.when(there)
        def _():
            pl.semaphore_signal(barrier, inc=1, device_id=(n, g + away), device_id_type=MESH)

    own = []
    for strip, ok in ((0, k > 0), (1, k >= 0), (2, k < STRIPS - 1)):
        rows_of = pl.ds(pl.multiple_of(OWN_X * (k + strip - 1), 16), OWN_X)
        for i, (src, part) in enumerate(((initial.at[:, :, rows_of, :], pl.ds(0, 2)), (feed.at[:, rows_of, :], 2))):
            own.append((ok, pltpu.make_async_copy(src, held.at[9 + strip, part], own_sem.at[strip, i])))
    for ok, copy in own:

        @pl.when(ok)
        def _():
            copy.start()

    pl.semaphore_wait(barrier, count)
    for ok, copy in own:

        @pl.when(ok)
        def _():
            copy.wait()

    exchange(held, first_sems, n, g, k, ((held.at[10, pl.ds(0, 3)], pl.ds(0, 3)),), False)

    refs = dict(held=held, sine=sine, sine_tenth=sine_tenth, coef=coef, power=power, state=state, rate=rate, modes=modes)
    device = Device(refs, g, k)
    u = device.step(held, True)
    for s in range(2):
        for z in range(OWN_Z):
            for t in range(2):
                at = u.at(s, Z_AT + z, X_AT + 8 * t)
                later[10, s, z, 8 * t : 8 * t + 8, :] = u.ref[pl.ds(at + M - 1, 8, stride=8), :]
    exchange(later, second_sems, n, g, k, ((later.at[10, pl.ds(0, 2)], pl.ds(0, 2)),), True)

    u = device.step(later, False)
    rows[...] = transform(u.ref[0 : volume(0), :], sine)

    def spread(m, _):
        for s in range(2):
            for z in range(OWN_Z):
                for t in range(2):
                    at = ((s * OWN_Z + z) * OWN_X + 8 * t) * 8
                    sending[m, s, z, 8 * t : 8 * t + 8, :] = rows[pl.ds(at + m, 8, stride=8), :]
        return 0

    lax.fori_loop(0, M, spread, 0)
    here = out.at[0, :, :, pl.ds(pl.multiple_of(OWN_X * k, 16), OWN_X), :]
    copies = []
    for j in range(1, M):
        to = (n + j) % M
        copy = remote(sending.at[to], here, send_sem.at[j], recv_sem.at[j], to, g)
        copy.start()
        copies.append(copy)
    local = pltpu.make_async_copy(sending.at[n], here, send_sem.at[0])
    local.start()
    local.wait()
    for copy in copies:
        copy.wait()


def on_device(initial, feed):
    sem = pltpu.SemaphoreType.DMA
    f32 = jnp.float32
    exchanges = [sem((3, 1)), sem((3, 1)), sem((4, 2)), sem((4, 2)), sem((3, 3)), sem((3, 3))]
    scratch = [
        pltpu.VMEM((21, 3, OWN_Z, OWN_X, WIDE), f32),
        pltpu.VMEM((21, 2, OWN_Z, OWN_X, WIDE), f32),
        pltpu.VMEM((volume(0), WIDE), f32),
        pltpu.VMEM((M, 2, OWN_Z, OWN_X, WIDE), f32),
        pltpu.VMEM((28 * 48 * 8, WIDE), f32),
    ]
    scratch += [pltpu.VMEM(((28 - 2 * i) * (40 - 2 * i) * 8, WIDE), f32) for i in range(1, 5)]
    scratch += [pltpu.VMEM((volume(d), WIDE), f32) for d in (8, 7, 7, 6)]
    scratch += [pltpu.VMEM((2 * 2 * 30 * 8, WIDE), f32), pltpu.VMEM((2 * 30 * 8, WIDE), f32)]
    scratch += [sem((3, 2))] + exchanges + exchanges + [sem((M,)), sem((M,))]
    vmem, anywhere = pl.BlockSpec(memory_space=pltpu.VMEM), pl.BlockSpec(memory_space=pl.ANY)
    return pl.pallas_call(
        kernel,
        out_shape=jax.ShapeDtypeStruct((1, 2, OWN_Z, WIDE, WIDE), f32),
        in_specs=[anywhere, anywhere, vmem, vmem, vmem],
        out_specs=anywhere,
        scratch_shapes=scratch,
        compiler_params=pltpu.CompilerParams(
            collective_id=0, has_side_effects=True, vmem_limit_bytes=60 * 1024 * 1024
        ),
    )(initial, feed, jnp.asarray(wide(SINE)), jnp.asarray(wide(0.1 * SINE)), jnp.asarray(COEF))


def solution(mesh):
    in_specs = (P(None, "gz", None, None), P("gz", None, None))
    out_specs = P("node", None, "gz", None, None)
    return jax.shard_map(on_device, mesh=mesh, in_specs=in_specs, out_specs=out_specs, check_vma=False)
```

time: 1050 us -> 98.4 us (0.09)
  waiting for transfers between devices: 829 us -> 0 us
  starting transfers between devices: 119 us -> 0 us
  Pallas kernels: 0 us -> 95.3 us
  matrix products: 48.9 us -> 0 us
  other arithmetic: 25.2 us -> 0 us
  between operations: 15.9 us -> 0.01 us
    all_gather x6 -> x0, waiting for transfers between devices: 550 us -> none  [on_device(): pieces = lax.all_gather(slopes, 'node', axis=0, tiled=True)]
    ppermute x48 -> x0, waiting for transfers between devices: 199 us -> none  [the longest x24 186 us: extended(): lax.ppermute(lax.slice_in_dim(block, block.shape[dim] - width, None, axis...]
    ppermute x48 -> x0, starting transfers between devices: 118 us -> none  [the longest x24 63.2 us: extended(): lax.ppermute(lax.slice_in_dim(block, 0, width, axis=dim), axis, backward)]
    pallas_call x0 -> x1, Pallas kernels: none -> 95.3 us  [on_device(): pl.pallas_call(kernel, out_shape=jax.ShapeDtypeStruct((1, 2, OWN_Z, WIDE,...]
    psum x1 -> x0, waiting for transfers between devices: 79.5 us -> none  [broadcast(): return lax.psum(jnp.where(mine, x, jnp.zeros_like(x)), axis)]
    dot_general x6 -> x0, matrix products: 48.9 us -> none  [on_device(): jnp.einsum('mj,jsabc->msabc', columns, pieces, precision=lax.Precision.HI...]
    add x6 -> x0, other arithmetic: 12.2 us -> none  [on_device(): slopes = diffusion * laplace + time_step * reaction(iterate, feed_rate)]
  transfers between devices with their start and end apart: 55 -> 0, of which waited for: 49 -> 0; matrix products, arithmetic and copies ran while one was open for 0% -> 0% of each run, Pallas kernels for 0% -> 0%
where the time goes in v1:
time: 98.4 us; the launch traced here: 97.2 us
  Pallas kernels  95.3 us (97%)
  local copies, waits for them, and re-layouts  1.87 us (2%)
    pallas_call x1, Pallas kernels, on_device(): pl.pallas_call(kernel, out_shape=jax.ShapeDtypeStruct((1, 2, OWN_Z, WIDE,...  95.3 us

profile of v1, /device:TPU:128, one launch (start us, length us, event | category | flops | bytes accessed | tf_op | source)
XLA Modules:
  0.0 97.2 jit_solution(1350004181884773668)
XLA Ops:
  0.0 95.3 %shard_map.55 = f32[1,2,4,128,128]{4,3,2,1,0:T(8,128)} custom-call(f32[2,4,128,128]{3,2,1,0:T(8,128)} %initial.1, f32[4,128,128]{2,1,0:T(8,128)} %feed.1, bf16[256,256]{1,0:T(8,128)(2,1)} %constant.6.clone.sine, bf16[256,256]{1,0:T(8,128)(2,1)} %constant.7.clone.sine_tenth, f32[312,128]{1,0:T(8,128)} %constant.8.clone.coef), custom_call_target="tpu_custom_call" | custom-call | tf_op jit(solution)/shard_map/pallas_call | solution.py:516
  95.4 1.9 %copy.7 = f32[1,2,4,128,128]{4,3,2,1,0:T(8,128)} copy(f32[1,2,4,128,128]{4,3,2,1,0:T(8,128)} %shard_map.55) | data formatting | bytes 1048576

commit v2 on v1

v2 whole, which is shorter than its diff:
```python
import math

import jax
import jax.numpy as jnp
import ml_dtypes
import numpy as np
from jax import lax
from jax.experimental import pallas as pl
from jax.experimental.pallas import tpu as pltpu
from jax.sharding import PartitionSpec as P

MESH = pl.DeviceIdType.MESH
M = 8
SLABS, STRIPS = 32, 8
OWN_Z, OWN_X = 4, 16
Z_AT, X_AT = 12, 16
SLOTS = 6
WIDE = 128


def legendre_pair(count, point):
    before = 1.0
    current = point
    for order in range(2, count + 1):
        after = ((2.0 * order - 1.0) * point * current - (order - 1.0) * before) / order
        before = current
        current = after
    return (current, before)


def radau_value(count, point):
    high, low = legendre_pair(count, point)
    return high - low


def radau_slope(count, point):
    high, low = legendre_pair(count, point)
    lower_high, lower_low = legendre_pair(count - 1, point)
    denom = point * point - 1.0
    slope_high = count * (point * high - low) / denom
    slope_low = (count - 1.0) * (point * lower_high - lower_low) / denom
    return slope_high - slope_low


def radau_tables(node_count):
    points = [1.0]
    for index in range(1, node_count):
        guess = math.cos(2.0 * math.pi * index / (2.0 * node_count - 1.0))
        for newton_index in range(100):
            guess = guess - radau_value(node_count, guess) / radau_slope(node_count, guess)
        points.append(guess)
    points = sorted(points)
    nodes = [(value + 1.0) / 2.0 for value in points]
    table = []
    for row in range(node_count):
        table.append([0.0] * node_count)
    for column in range(node_count):
        coeffs = [1.0]
        for other in range(node_count):
            if other != column:
                factor = 1.0 / (nodes[column] - nodes[other])
                shifted = [0.0] + coeffs
                scaled = [-nodes[other] * value for value in coeffs] + [0.0]
                coeffs = [(shifted[k] + scaled[k]) * factor for k in range(len(shifted))]
        for row in range(node_count):
            total = 0.0
            for power in range(len(coeffs)):
                total = total + coeffs[power] * nodes[row] ** (power + 1) / (power + 1.0)
            table[row][column] = total
    return (nodes, table)


def tables():
    nodes, weights = radau_tables(M)
    t, q = np.asarray(nodes), np.asarray(weights)
    k = np.arange(1, WIDE + 1)
    sine = np.sqrt(2.0 / (WIDE + 1)) * np.sin(np.pi * np.outer(k, k) / (WIDE + 1))
    index, rows = {}, []

    def add(name, column):
        index[name] = len(rows)
        rows.append(np.broadcast_to(column[:, None], (8, WIDE)))

    index["lam"] = 0
    rows.append(np.broadcast_to(2.0 * np.cos(np.pi * k / (WIDE + 1))[None, :], (8, WIDE)))
    for s, nu in ((0, 1.0), (1, 2.0)):
        c = t * nu
        i = 1.0 / (1.0 + 6.0 * c)
        a = c * i
        for p in range(4):
            add(("A", s, p), a**p * i * ((1.0 - 0.1 * t) if s == 0 else 1.0))
            add(("N", s, p), a**p * i * t * (1.0 if s == 0 else -1.0))
        add(("A", s, 4), a**4)
        for sweep in (2, 3):
            c = t * nu / sweep
            i = 1.0 / (1.0 + 6.0 * c)
            add(("i", s, sweep), i)
            add(("a", s, sweep), c * i)
            for j in range(M):
                add(("q", s, sweep, j), i * q[:, j])
    return np.concatenate(rows, 0).astype(np.float32), index, sine


COEF, INDEX, SINE = tables()


def wide(matrix):
    high = matrix.astype(ml_dtypes.bfloat16)
    low = (matrix - high.astype(np.float64)).astype(ml_dtypes.bfloat16)
    return np.block([[high, low], [high, np.zeros_like(low)]]).astype(ml_dtypes.bfloat16)


def transform(v, matrix):
    high = v.astype(jnp.bfloat16)
    low = (v - high.astype(jnp.float32)).astype(jnp.bfloat16)
    both = jnp.dot(jnp.concatenate([high, low], 1), matrix[...], preferred_element_type=jnp.float32)
    return both[:, :WIDE] + both[:, WIDE:]


def total(terms):
    while len(terms) > 1:
        odd = [terms[-1]] if len(terms) % 2 else []
        terms = [terms[i] + terms[i + 1] for i in range(0, len(terms) - 1, 2)] + odd
    return terms[0]


class Stack:
    def __init__(self, ref, z0, nz, x0, nx):
        self.ref, self.z0, self.nz, self.x0, self.nx = ref, z0, nz, x0, nx
        self.lines = {}

    def start(self, s, z):
        if isinstance(z, int):
            return (s * self.nz + z - self.z0) * self.nx * 8
        if (s, id(z)) not in self.lines:
            self.lines[s, id(z)] = z, (z + (s * self.nz - self.z0)) * (self.nx * 8)
        return self.lines[s, id(z)][1]

    def at(self, s, z, x, dz=0):
        return pl.multiple_of(self.start(s, z) + (dz * self.nx + x - self.x0) * 8, 8)

    def get(self, s, z, x, dz=0):
        return self.ref[pl.ds(self.at(s, z, x, dz), 8), :]

    def put(self, s, z, x, v):
        self.ref[pl.ds(self.at(s, z, x), 8), :] = v

    def row(self, s, z, x, f):
        return jnp.broadcast_to(self.ref[pl.ds(self.at(s, z, x) + f, 1), :], (8, WIDE))

    def line(self, s, z, x, n):
        return self.ref[pl.ds(self.at(s, z, x), n * 8), :]


def span(depth):
    layers = OWN_Z + (2 * depth if depth < 4 else depth + (depth - 4))
    return (Z_AT - depth, layers, X_AT - depth, OWN_X + 2 * depth)


def volume(depth):
    _, layers, _, columns = span(depth)
    return 2 * layers * columns * 8


class Device:
    def __init__(self, refs, g, k):
        self.__dict__.update(refs)
        self.k, self.core = k, g % 2
        self.far = g // 2 + self.core * (SLABS // 2 - 1 - 2 * (g // 2))

    def zero_packed(self, stack):
        for edge, x in ((0, X_AT - 1), (STRIPS - 1, X_AT + OWN_X)):

            @pl.when(self.k == edge)
            def _():
                def body(z, _):
                    stack.put(0, z, x, jnp.zeros((8, WIDE), jnp.float32))
                    return 0

                lax.fori_loop(stack.z0, stack.z0 + stack.nz, body, 0)

        for edge, z in ((0, Z_AT - 1), (1, Z_AT - 9), (SLABS // 2 - 1, Z_AT + 8)):

            @pl.when(self.far == edge)
            def _():
                for half in range(2):
                    line = z - 8 * half
                    if stack.z0 <= line < stack.z0 + stack.nz:

                        def body(x, _):
                            stack.ref[pl.ds(stack.at(0, line, x) + 4 * half, 4), :] = jnp.zeros((4, WIDE), jnp.float32)
                            return 0

                        lax.fori_loop(stack.x0, stack.x0 + stack.nx, body, 0)

    def natural(self, layer):
        return layer + self.core * (OWN_Z - 1 - 2 * layer)

    def co(self, name):
        i = INDEX[name]
        return self.coef[i * 8 : (i + 1) * 8, :]

    def zero_edges(self, stack, species=(0, 1), lines=None):
        first, last = lines or (stack.z0, stack.z0 + stack.nz)
        for edge, x in ((0, X_AT - 1), (STRIPS - 1, X_AT + OWN_X)):

            @pl.when(self.k == edge)
            def _():
                def body(z, _):
                    for s in species:
                        stack.put(s, z, x, jnp.zeros((8, WIDE), jnp.float32))
                    return 0

                lax.fori_loop(first, last, body, 0)

        for edge, z in ((0, Z_AT - 1), (1, Z_AT - 9), (SLABS // 2 - 1, Z_AT + 8)):
            if first <= z < last:

                @pl.when(self.far == edge)
                def _():
                    for s in species:
                        stack.ref[pl.ds(stack.at(s, z, stack.x0), stack.nx * 8), :] = jnp.zeros(
                            (stack.nx * 8, WIDE), jnp.float32
                        )

    def load(self, blocks, first, stack, slot):
        b = slot * 3
        x = jnp.concatenate([blocks[b + i, 0:2].reshape(128, WIDE) for i in range(3)], 0)
        y = transform(x, self.sine)
        real, spec = (x, y) if first else (y, x)
        n = []
        for i in range(3):
            p, q = real[i * 128 : i * 128 + 64], real[i * 128 + 64 : i * 128 + 128]
            feed = self.held[b + i, 2].reshape(64, WIDE)
            n.append((1.0 + p) * (q + p * (feed + q)))
        n = transform(jnp.concatenate(n, 0), self.sine_tenth)
        for half in range(2):
            if not 0 <= slot - 2 * half < 4:
                continue
            for i in range(3):
                for layer in range(4):
                    for t in range(2):
                        z = (slot - 2 * half) * 4 + self.natural(layer)
                        at = stack.at(0, z, i * 16 + t * 8) + 4 * half
                        r = layer * 16 + t * 8
                        for f, v in (
                            (0, spec[i * 128 + r : i * 128 + r + 8]),
                            (1, spec[i * 128 + 64 + r : i * 128 + 64 + r + 8]),
                            (2, n[i * 64 + r : i * 64 + r + 8]),
                        ):
                            stack.ref[pl.ds(at + f, 8, stride=8), :] = v

    def apply_s(self, src, dst):
        lam = self.co("lam")

        def body(z, _):
            for x0 in range(dst.x0, dst.x0 + dst.nx, 8):
                xs = range(x0, min(x0 + 8, dst.x0 + dst.nx))
                row = {x: src.get(0, z, x) for x in range(xs[0] - 1, xs[-1] + 2)}
                for x in xs:
                    zx = (row[x - 1] + row[x + 1]) + (src.get(0, z, x, -1) + src.get(0, z, x, 1))
                    dst.put(0, z, x, zx + lam * row[x])
            return 0

        lax.fori_loop(dst.z0, dst.z0 + dst.nz, body, 0)

    def combine(self, powers, out):
        ca = [[self.co(("A", s, p)) for p in range(5)] for s in range(2)]
        cn = [[self.co(("N", s, p)) for p in range(4)] for s in range(2)]
        def body(z, _):
            half = lax.div(z - 4, 8)
            line, row = z - 8 * half, 4 * half
            for x in range(out.x0, out.x0 + out.nx):
                n = [powers[p].row(0, line, x, row + 2) for p in range(4)]
                for s in range(2):
                    terms = [ca[s][p] * powers[p].row(0, line, x, row + s) for p in range(5)]
                    out.put(s, z, x, total(terms + [cn[s][p] * n[p] for p in range(4)]))
            return 0

        lax.fori_loop(out.z0, out.z0 + out.nz, body, 0)

    def rates(self, u, anchor, right, out, sweep, pause=None):
        lam = self.co("lam")
        a, inv = [[self.co((name, s, sweep)) for s in range(2)] for name in "ai"]
        a6 = [6.0 * a[s] for s in range(2)]
        weights = [[self.co(("q", s, sweep, j)) for j in range(M)] for s in range(2)]
        nx, x0, lines = right.nx, right.x0, right.nz
        lam6, lam61 = lam - 6.0, lam - 6.1
        rate = Stack(self.rate, 0, 1, x0, nx)

        def nonlinear(i, place):
            z = right.z0 + lax.rem(i, lines)
            real = transform(jnp.concatenate([u.line(s, z, x0, nx) for s in range(2)], 0), self.sine)
            feed = []
            for x in range(x0, x0 + nx):
                line = self.held[(z // 4) * 3 + x // 16, 2, self.natural(z % 4), pl.ds(x % 16, 1), :]
                feed.append(jnp.broadcast_to(line, (8, WIDE)))
            feed = jnp.concatenate(feed, 0)
            p, q = real[: nx * 8], real[nx * 8 :]
            self.reals[place][0 : nx * 8, :] = (1.0 + p) * (q + p * (feed + q))

        def modes(place):
            self.modes[place][0 : nx * 8, :] = transform(self.reals[place][0 : nx * 8, :], self.sine_tenth)

        def sums(i, place):
            z = right.z0 + i
            row = [{x: u.get(s, z, x) for x in range(x0 - 1, x0 + nx + 1)} for s in range(2)]
            half = lax.div(z - 4, 8)
            line = z - 8 * half
            for x in range(x0, x0 + nx):
                laplace = []
                for s in range(2):
                    zx = (row[s][x - 1] + row[s][x + 1]) + (u.get(s, z, x, -1) + u.get(s, z, x, 1))
                    laplace.append(zx + lam6 * row[s][x])
                    if s == 0:
                        drift = zx + lam61 * row[s][x]
                n = self.modes[place][(x - x0) * 8 : (x - x0) * 8 + 8, :]
                rate.put(0, 0, x, drift + n)
                rate.put(1, 0, x, 2.0 * laplace[1] - n)
                for s in range(2):
                    integral = total([weights[s][j] * rate.row(s, 0, x, j) for j in range(M)])
                    base = inv[s] * anchor.row(0, line, x, 4 * half + s) + integral
                    right.put(s, z, x, base - a[s] * laplace[s])
                    out.put(s, z, x, base + a6[s] * row[s][x])

        nonlinear(jnp.int32(0), 0)
        nonlinear(jnp.int32(1), 1)
        modes(0)

        def body(h, _):
            for place in range(2):
                i = 2 * h + place
                nonlinear(i + 2, place)
                modes(1 - place)
                sums(i, place)
            return 0

        ready = 0
        if pause is not None:
            ready = 2
            lax.fori_loop(0, ready, body, 0)
            pause()
        lax.fori_loop(ready, lines // 2, body, 0)

    def jacobi(self, src, right, dst, sweep, lines, species):
        lam = self.co("lam")
        a = [self.co(("a", s, sweep)) for s in range(2)]

        def body(z, _):
            for x0 in range(dst.x0, dst.x0 + dst.nx, 7):
                xs = range(x0, min(x0 + 7, dst.x0 + dst.nx))
                for s in species:
                    row = {x: src.get(s, z, x) for x in range(xs[0] - 1, xs[-1] + 2)}
                    for x in xs:
                        zx = (row[x - 1] + row[x + 1]) + (src.get(s, z, x, -1) + src.get(s, z, x, 1))
                        dst.put(s, z, x, right.get(s, z, x) + a[s] * (zx + lam * row[x]))
            return 0

        lax.fori_loop(*lines, body, 0)

    def layout(self):
        powers = [Stack(self.power[0], 0, 16, 0, 48)]
        powers += [Stack(self.power[i], i, 16 - 2 * i, 4 + i, 40 - 2 * i) for i in range(1, 5)]
        return powers, Stack(self.state[0], *span(8))

    def iterate(self, out, right, sweep, depth, dst, species=(0, 1)):
        for d, place in ((depth - 2, 3), (depth - 3, 2), (depth - 4, None)):
            to = dst if place is None else Stack(self.state[place], *span(d))
            self.zero_edges(out, species)
            z0, layers, _, _ = span(d)
            self.jacobi(out, right, to, sweep, (z0, z0 + layers), species)
            out = to

    def step(self, half, share):
        powers, u = self.layout()
        for i in range(4):
            self.zero_packed(powers[i])
            self.apply_s(powers[i], powers[i + 1])
        self.combine(powers, u)
        right, out = Stack(self.state[1], *span(7)), Stack(self.state[2], *span(7))
        self.zero_edges(u)
        self.rates(u, powers[0], right, out, 2)
        u = self.second(half)
        self.iterate(out, right, 2, 8, u)
        self.zero_edges(u, lines=(Z_AT - 4, Z_AT + OWN_Z))
        pause = share(u)
        right, out = Stack(self.state[1], *span(3)), Stack(self.state[2], *span(3))
        self.rates(u, powers[0], right, out, 3, pause)
        return right, out, Stack(self.state[0], *span(0))

    def second(self, half):
        return Stack(half, Z_AT - 4, 12, X_AT - 4, OWN_X + 8)


def strip_of(node):
    y = node // 2
    return 2 * y + (node + y) % 2


class Links:
    def __init__(self):
        self.sent = []

    def send(self, when, copy):
        @pl.when(when)
        def _():
            copy.start()

        self.sent.append((when, copy))

    def finish(self):
        for when, copy in self.sent:

            @pl.when(when)
            def _():
                copy.wait_send()


def remote(src, dst, sent, got, node, g):
    return pltpu.make_async_remote_copy(
        src_ref=src, dst_ref=dst, send_sem=sent, recv_sem=got, device_id=(node, g), device_id_type=MESH
    )


def arrive(when, copy):
    @pl.when(when)
    def _():
        copy.wait_recv()


def exchange(held, sems, n, g, k, own_parts, strips_too, load):
    zs, zr, xs, xr, ss, sr = sems
    links = Links()
    tau = 2 * (g % 2) - 1
    partner = g - tau
    low, high = k > 0, k < STRIPS - 1

    def inside(i):
        return jnp.logical_and(i >= 0, i < SLABS)

    def block(slot, strip):
        return held.at[slot * 3 + strip]

    for d, away in ((1, tau), (2, -2 * tau), (3, 3 * tau)):
        for i, (src, part) in enumerate(own_parts):
            copy = remote(src, held.at[(3 - d) * 3 + 1, part], zs.at[d - 1, i], zr.at[d - 1, i], n, g + away)
            links.send(inside(g + away), copy)

    def along_x(j, there):
        for way, (ok, to, strip) in enumerate(((high, k + 1, 0), (low, k - 1, 2))):
            copy = remote(block(3 - j, 1), block(3 - j, strip), xs.at[j, way], xr.at[j, way], strip_of(to), g)
            links.send(jnp.logical_and(ok, there), copy)

    def swap(j, strip, there):
        copy = remote(block(3 - j, strip), block(4 + j, strip), ss.at[j, strip], sr.at[j, strip], n, partner)
        links.send(there, copy)

    def from_z(j):
        there = inside(g + tau * j)
        for i, (src, part) in enumerate(own_parts):
            arrive(there, remote(src, held.at[(3 - j) * 3 + 1, part], zs.at[j - 1, i], zr.at[j - 1, i], n, partner))
        along_x(j, there)
        if j < 2:
            swap(j, 1, there)

    def from_x(j):
        there = inside(g + tau * j)
        for way, (ok, strip) in enumerate(((low, 0), (high, 2))):
            when = jnp.logical_and(ok, there)
            got = block(3 - j, strip)
            arrive(when, remote(got, got, xs.at[j, way], xr.at[j, way], n, partner))
            if j < 2:
                swap(j, strip, when)

    def from_partner(j):
        there = inside(g - tau * (j + 1))
        for strip, ok in ((0, low), (1, always), (2, high)):
            got = block(4 + j, strip)
            arrive(jnp.logical_and(ok, there), remote(got, got, ss.at[j, strip], sr.at[j, strip], n, partner))

    always = g >= 0
    swap(0, 1, always)
    if strips_too:
        along_x(0, always)
        from_x(0)
        from_z(1)
        load(3)
    else:
        swap(0, 0, low)
        swap(0, 2, high)
        load(3)
        from_z(1)
    from_z(2)
    from_z(3)
    from_x(1)
    from_partner(0)
    load(2)
    load(4)
    from_x(2)
    load(1)
    from_partner(1)
    load(5)
    from_x(3)
    load(0)
    links.finish()


def refs_of(held, consts, scratch):
    sine, sine_tenth, coef = consts
    return dict(
        held=held, sine=sine, sine_tenth=sine_tenth, coef=coef,
        power=scratch[0:5], state=scratch[5:9], rate=scratch[9], reals=scratch[10:12], modes=scratch[12:14],
    )


def constants():
    return wide(SINE), wide(0.1 * SINE), COEF


def compute_scratch():
    f32 = jnp.float32
    scratch = [pltpu.VMEM((16 * 48 * 8, WIDE), f32)]
    scratch += [pltpu.VMEM(((16 - 2 * i) * (40 - 2 * i) * 8, WIDE), f32) for i in range(1, 5)]
    scratch += [pltpu.VMEM((volume(d), WIDE), f32) for d in (8, 7, 7, 6)]
    return scratch + [pltpu.VMEM((2 * 30 * 8, WIDE), f32)] + [pltpu.VMEM((30 * 8, WIDE), f32)] * 4 + [pltpu.VMEM((2 * 12 * 24 * 8, WIDE), f32)] * 2


def kernel(initial, feed, *rest):
    consts, (out, held, later, rows, sending) = rest[0:3], rest[3:8]
    scratch, sems = rest[8:-19], rest[-19:]
    sine = consts[0]
    own_sem, first_sems, second_sems, (send_sem, recv_sem), shares = sems[0], sems[1:7], sems[7:13], sems[13:15], sems[15:19]
    n, g = lax.axis_index("node"), lax.axis_index("gz")
    k = strip_of(n)
    tau = 2 * (g % 2) - 1

    barrier = pltpu.get_barrier_semaphore()
    count = M - 1
    for j in range(1, M):
        pl.semaphore_signal(barrier, inc=1, device_id=((n + j) % M, g), device_id_type=MESH)
    for away in (-2 * tau, -tau, tau, 2 * tau, 3 * tau):
        there = jnp.logical_and(g + away >= 0, g + away < SLABS)
        count = count + jnp.where(there, 1, 0)

        @pl.when(there)
        def _():
            pl.semaphore_signal(barrier, inc=1, device_id=(n, g + away), device_id_type=MESH)

    own = []
    for strip, ok in ((0, k > 0), (1, k >= 0), (2, k < STRIPS - 1)):
        rows_of = pl.ds(pl.multiple_of(OWN_X * (k + strip - 1), 16), OWN_X)
        for i, (src, part) in enumerate(((initial.at[:, :, rows_of, :], pl.ds(0, 2)), (feed.at[:, rows_of, :], 2))):
            own.append((ok, pltpu.make_async_copy(src, held.at[9 + strip, part], own_sem.at[strip, i])))
    for ok, copy in own:

        @pl.when(ok)
        def _():
            copy.start()

    pl.semaphore_wait(barrier, count)
    for ok, copy in own:

        @pl.when(ok)
        def _():
            copy.wait()

    device = Device(refs_of(held, consts, scratch), g, k)
    powers, _ = device.layout()

    def load(blocks, first):
        return lambda slot: device.load(blocks, first, powers[0], slot)

    parts = pl.ds(0, 3)
    exchange(held, first_sems, n, g, k, ((held.at[10, parts], parts),), False, load(held, True))
    halves = scratch[14:16]

    def share(i):
        def start(u):
            copies = []
            for s in range(2):
                for z in range(OWN_Z):
                    src = u.ref.at[pl.ds(u.at(s, Z_AT + z, u.x0), u.nx * 8), :]
                    dst = u.ref.at[pl.ds(u.at(s, Z_AT + 7 - z, u.x0), u.nx * 8), :]
                    place = s * OWN_Z + z
                    copies.append(remote(src, dst, shares[2 * i].at[place], shares[2 * i + 1].at[place], n, g - tau))
            for copy in copies:
                copy.start()

            def wait():
                for copy in copies:
                    copy.wait()

            return wait

        return start

    right, iterate, u = device.step(halves[0], share(0))
    device.iterate(iterate, right, 3, 4, u)
    for s in range(2):
        for z in range(OWN_Z):
            for t in range(2):
                at = u.at(s, Z_AT + device.natural(z), X_AT + 8 * t)
                later[10, s, z, 8 * t : 8 * t + 8, :] = u.ref[pl.ds(at + M - 1, 8, stride=8), :]
    parts = pl.ds(0, 2)
    exchange(later, second_sems, n, g, k, ((later.at[10, parts], parts),), True, load(later, False))

    right, iterate, u = device.step(halves[1], share(1))
    copies = []
    for s in range(2):
        device.iterate(iterate, right, 3, 4, u, (s,))
        rows[...] = transform(u.ref[s * volume(0) // 2 : (s + 1) * volume(0) // 2, :], sine)

        def spread(m, _):
            for z in range(OWN_Z):
                for t in range(2):
                    at = pl.multiple_of((device.natural(z) * OWN_X + 8 * t) * 8, 8)
                    sending[m, s, z, 8 * t : 8 * t + 8, :] = rows[pl.ds(at + m, 8, stride=8), :]
            return 0

        lax.fori_loop(0, M, spread, 0)
        here = out.at[0, s, :, pl.ds(pl.multiple_of(OWN_X * k, 16), OWN_X), :]
        for j in (4, 3, 5, 2, 6, 1, 7):
            to = (n + j) % M
            copies.append(remote(sending.at[to, s], here, send_sem.at[s, j], recv_sem.at[s, j], to, g))
            copies[-1].start()
        copies.append(pltpu.make_async_copy(sending.at[n, s], here, send_sem.at[s, 0]))
        copies[-1].start()
    for copy in copies:
        copy.wait()


def on_device(initial, feed):
    sem = pltpu.SemaphoreType.DMA
    f32 = jnp.float32
    exchanges = [sem((3, 1)), sem((3, 1)), sem((4, 2)), sem((4, 2)), sem((2, 3)), sem((2, 3))]
    scratch = [
        pltpu.VMEM((3 * SLOTS, 3, OWN_Z, OWN_X, WIDE), f32),
        pltpu.VMEM((3 * SLOTS, 2, OWN_Z, OWN_X, WIDE), f32),
        pltpu.VMEM((volume(0) // 2, WIDE), f32),
        pltpu.VMEM((M, 2, OWN_Z, OWN_X, WIDE), f32),
    ]
    scratch += compute_scratch()
    scratch += [sem((3, 2))] + exchanges + exchanges + [sem((2, M)), sem((2, M))] + [sem((2 * OWN_Z,))] * 4
    vmem, anywhere = pl.BlockSpec(memory_space=pltpu.VMEM), pl.BlockSpec(memory_space=pl.ANY)
    return pl.pallas_call(
        kernel,
        out_shape=jax.ShapeDtypeStruct((1, 2, OWN_Z, WIDE, WIDE), f32),
        in_specs=[anywhere, anywhere] + [vmem] * 3,
        out_specs=anywhere,
        scratch_shapes=scratch,
        compiler_params=pltpu.CompilerParams(
            collective_id=0, has_side_effects=True, vmem_limit_bytes=60 * 1024 * 1024
        ),
    )(initial, feed, *[jnp.asarray(c) for c in constants()])


def solution(mesh):
    in_specs = (P(None, "gz", None, None), P("gz", None, None))
    out_specs = P("node", None, "gz", None, None)
    return jax.shard_map(on_device, mesh=mesh, in_specs=in_specs, out_specs=out_specs, check_vma=False)
```

time: 98.4 us -> 81 us (0.82); the launches traced: 97.2 us -> 80.9 us
  Pallas kernels: 95.3 us -> 79 us
    pallas_call x1, Pallas kernels: 95.3 us -> 79 us  [on_device(): pl.pallas_call(kernel, out_shape=jax.ShapeDtypeStruct((1, 2, OWN_Z, WIDE,...]
where the time goes in v2:
time: 81 us; the launch traced here: 80.9 us
  Pallas kernels  79 us (98%)
  local copies, waits for them, and re-layouts  1.87 us (2%)
    pallas_call x1, Pallas kernels, on_device(): pl.pallas_call(kernel, out_shape=jax.ShapeDtypeStruct((1, 2, OWN_Z, WIDE,...  79 us
    unnamed x1, local copies, waits for them, and re-layouts  1.87 us

profile of v2, /device:TPU:128, one launch (start us, length us, event | category | flops | bytes accessed | tf_op | source)
XLA Modules:
  0.0 80.9 jit_solution(15495945098410417269)
XLA Ops:
  0.0 79.0 %shard_map.55 = f32[1,2,4,128,128]{4,3,2,1,0:T(8,128)} custom-call(f32[2,4,128,128]{3,2,1,0:T(8,128)} %initial.1, f32[4,128,128]{2,1,0:T(8,128)} %feed.1, bf16[256,256]{1,0:T(8,128)(2,1)} %constant.6.clone.rest_0_, bf16[256,256]{1,0:T(8,128)(2,1)} %constant.7.clone.rest_1_, f32[472,128]{1,0:T(8,128)} %constant.8.clone.rest_2_), custom_call_target="tpu_custom_call" | custom-call | tf_op jit(solution)/shard_map/pallas_call | solution.py:645
  79.0 1.9 %copy.7 = f32[1,2,4,128,128]{4,3,2,1,0:T(8,128)} copy(f32[1,2,4,128,128]{4,3,2,1,0:T(8,128)} %shard_map.55) | data formatting | bytes 1048576

commit v3 on v2

--- a/solution.py
+++ b/solution.py
@@ -519,7 +519,7 @@
 
 def compute_scratch():
     f32 = jnp.float32
-    scratch = [pltpu.VMEM((16 * 48 * 8, WIDE), f32)]
+    scratch = [pltpu.VMEM((16 * 48 * 8 + 8, WIDE), f32)]
     scratch += [pltpu.VMEM(((16 - 2 * i) * (40 - 2 * i) * 8, WIDE), f32) for i in range(1, 5)]
     scratch += [pltpu.VMEM((volume(d), WIDE), f32) for d in (8, 7, 7, 6)]
     return scratch + [pltpu.VMEM((2 * 30 * 8, WIDE), f32)] + [pltpu.VMEM((30 * 8, WIDE), f32)] * 4 + [pltpu.VMEM((2 * 12 * 24 * 8, WIDE), f32)] * 2
@@ -608,7 +608,7 @@
     copies = []
     for s in range(2):
         device.iterate(iterate, right, 3, 4, u, (s,))
-        rows[...] = transform(u.ref[s * volume(0) // 2 : (s + 1) * volume(0) // 2, :], sine)
+        rows[0 : volume(0) // 2, :] = transform(u.ref[s * volume(0) // 2 : (s + 1) * volume(0) // 2, :], sine)
 
         def spread(m, _):
             for z in range(OWN_Z):
@@ -636,7 +636,7 @@
     scratch = [
         pltpu.VMEM((3 * SLOTS, 3, OWN_Z, OWN_X, WIDE), f32),
         pltpu.VMEM((3 * SLOTS, 2, OWN_Z, OWN_X, WIDE), f32),
-        pltpu.VMEM((volume(0) // 2, WIDE), f32),
+        pltpu.VMEM((volume(0) // 2 + 8, WIDE), f32),
         pltpu.VMEM((M, 2, OWN_Z, OWN_X, WIDE), f32),
     ]
     scratch += compute_scratch()

time: 81 us -> 81.4 us (level)
  no operation moved by 1% of the time
where the time goes in v3:
time: 81.4 us; the launch traced here: 81.3 us
  Pallas kernels  79.4 us (98%)
  local copies, waits for them, and re-layouts  1.87 us (2%)
    pallas_call x1, Pallas kernels, on_device(): pl.pallas_call(kernel, out_shape=jax.ShapeDtypeStruct((1, 2, OWN_Z, WIDE,...  79.4 us
    unnamed x1, local copies, waits for them, and re-layouts  1.87 us

profile of v3, /device:TPU:128, one launch (start us, length us, event | category | flops | bytes accessed | tf_op | source)
XLA Modules:
  0.0 81.3 jit_solution(7477765913293454788)
XLA Ops:
  0.0 79.4 %shard_map.55 = f32[1,2,4,128,128]{4,3,2,1,0:T(8,128)} custom-call(f32[2,4,128,128]{3,2,1,0:T(8,128)} %initial.1, f32[4,128,128]{2,1,0:T(8,128)} %feed.1, bf16[256,256]{1,0:T(8,128)(2,1)} %constant.6.clone.rest_0_, bf16[256,256]{1,0:T(8,128)(2,1)} %constant.7.clone.rest_1_, f32[472,128]{1,0:T(8,128)} %constant.8.clone.rest_2_), custom_call_target="tpu_custom_call" | custom-call | tf_op jit(solution)/shard_map/pallas_call | solution.py:645
  79.4 1.9 %copy.7 = f32[1,2,4,128,128]{4,3,2,1,0:T(8,128)} copy(f32[1,2,4,128,128]{4,3,2,1,0:T(8,128)} %shard_map.55) | data formatting | bytes 1048576
